TPU v7x, 128 devices: a whole 4x4x4 slice. The times are simulated.
128 devices in a mesh: fsdp: 16 (over y_lo, z, core), tp: 8 (over x, y_hi).
Axes of the slice: x: 4, y: 4 (y_hi: 2, y_lo: 2; y = y_hi * 2 + y_lo), z: 4, core: 2. Of those that a mesh axis runs over, the one named last changes fastest.
Arguments:
- hidden_in: bfloat16 [1024, 4096], P('fsdp'), may hold values from -3 to 3
- queries: bfloat16 [2, 1024, 8192], P(None, ('fsdp', 'tp')), may hold values from -170 to 170
- key_cache: bfloat16 [1024, 256, 512], P(('fsdp', 'tp')), may hold values from -6 to 6
- value_cache: bfloat16 [1024, 256, 512], P(('fsdp', 'tp')), may hold values from -6 to 6
- new_keys: bfloat16 [2, 1024, 512], P(None, ('fsdp', 'tp')), may hold values from -6 to 6
- new_values: bfloat16 [2, 1024, 512], P(None, ('fsdp', 'tp')), may hold values from -6 to 6
- lengths: int32 [1024], P(('fsdp', 'tp')), may hold values from 2 to 256
- routes: int32 [2, 1024, 8], P(None, 'fsdp'), may hold values from 0 to 127, all different within a row; in each aligned block of 64 rows (0 to 63, 64 to 127, ..., all dimensions but the last counted through in order) at most 8 rows name the same one
- route_weights: float32 [2, 1024, 8], P(None, 'fsdp'), may hold values from 0.05 to 1
- norm_gain: float32 [4096], replicated, may hold values from 0.1 to 1.9
- gate_master: float32 [8, 1536, 4096], P(None, ('fsdp', 'tp')), may hold values from -0.09375 to 0.09375
- up_master: float32 [8, 1536, 4096], P(None, ('fsdp', 'tp')), may hold values from -0.09375 to 0.09375
- down_master: float32 [8, 1536, 4096], P(None, ('fsdp', 'tp')), may hold values from -0.3125 to 0.3125
- out_proj: bfloat16 [8192, 4096], P('tp'), may hold values from -0.0625 to 0.0625
Outputs:
- hidden_out: bfloat16 [1024, 4096], P('fsdp', 'tp')
- scale_log2: float32 [3, 8, 12, 32], replicated
Inputs may be any that keep to these rules, and one draw needn't show every extreme that they name: `routes`: within one step and one index of fsdp (aligned blocks of 64 rows), no expert is named by more than 8 rows.
All inputs are finite; a program needn't handle non-finite values.
Results may differ from a plain program's by a relative error of at most 0.0095.
Values may be sent and summed in bfloat16 or wider, within the bound.
A program may use at most 256 MiB of HBM per device.

v0:
```python
import jax
import jax.numpy as jnp
from jax import lax
from jax.sharding import PartitionSpec as P

D = 4096
FF = 1536
QH = 64
KVH = 4
HD = 128
BLOCK = 128
WIN = 8
CAP = 8
neg_fill = -1e30
epsilon = 1e-06
fp_limit = 448.0
grid_floor = 2.0 ** (-10)
least_exponent = -6.0


def cut_along(array, dim, peers):
    before, after = (array.shape[:dim], array.shape[dim + 1 :])
    return jnp.moveaxis(array.reshape(*before, peers, -1, *after), dim, 0)


def sent_and_summed(array, axis, dim):
    blocks = cut_along(array, dim, lax.axis_size(axis))
    arrived = lax.all_to_all(blocks, axis, split_axis=0, concat_axis=0, tiled=True)
    return arrived.astype(jnp.float32).sum(axis=0)


def copy_for_each(array, axis):
    peers = lax.axis_size(axis)
    return lax.all_to_all(
        jnp.broadcast_to(array[None], (peers, *array.shape)), axis, 0, 0, tiled=True
    )


def joined_along(blocks, dim):
    blocks = jnp.moveaxis(blocks, 0, dim)
    lengths = blocks.shape
    return blocks.reshape(*lengths[:dim], lengths[dim] * lengths[dim + 1], *lengths[dim + 2 :])


def collect(array, axis, dim):
    blocks = copy_for_each(array, axis)
    return joined_along(blocks, dim)


def grid_round(values):
    magnitude = jnp.abs(values)
    exponent = jnp.maximum(jnp.floor(jnp.log2(jnp.maximum(magnitude, grid_floor))), least_exponent)
    spacing = jnp.exp2(exponent - 3.0)
    return jnp.sign(values) * jnp.floor(magnitude / spacing + 0.5) * spacing


def row_scales(scales, owner_map):
    return jnp.einsum(
        "sb,xwbc->xwsc", owner_map.astype(jnp.float32), scales, precision=lax.Precision.HIGHEST
    )


def owner_blocks(owner_rows):
    return (owner_rows // BLOCK)[:, None] == jnp.arange(FF // BLOCK, dtype=jnp.int32)[None, :]


def dequantize(shard_piece, shard_rows, tp_count, tp_pos, scales):
    count = shard_piece.shape[2]
    gathered_index = jnp.arange(count, dtype=jnp.int32)
    owner_rows = (
        gathered_index // shard_rows * tp_count + tp_pos
    ) * shard_rows + gathered_index % shard_rows
    factors = row_scales(scales, owner_blocks(owner_rows))
    tiles = shard_piece.astype(jnp.float32).reshape(3, WIN, count, D // BLOCK, BLOCK)
    return (tiles * factors[..., None]).astype(jnp.bfloat16).reshape(3, WIN, count, D)


def attention_rows(queries_now, cache_keys, cache_values, fresh_keys, fresh_values, lengths):
    row_count = queries_now.shape[0]
    positions = cache_keys.shape[1]
    group = QH // KVH
    score_scale = HD ** (-0.5)
    fresh_count = fresh_keys.shape[0]
    query_heads = queries_now.reshape(row_count, KVH, group, HD)
    key_heads = cache_keys.reshape(row_count, positions, KVH, HD)
    value_heads = cache_values.reshape(row_count, positions, KVH, HD)
    fresh_key_heads = fresh_keys.reshape(fresh_count, row_count, KVH, HD)
    fresh_value_heads = fresh_values.reshape(fresh_count, row_count, KVH, HD)
    cached_scores = (
        jnp.einsum("rkgd,rpkd->rkgp", query_heads, key_heads, preferred_element_type=jnp.float32)
        * score_scale
    )
    fresh_scores = (
        jnp.einsum(
            "rkgd,srkd->rkgs", query_heads, fresh_key_heads, preferred_element_type=jnp.float32
        )
        * score_scale
    )
    alive_mask = (jnp.arange(positions, dtype=jnp.int32)[None, :] < lengths[:, None])[
        :, None, None, :
    ]
    peak_score = jnp.maximum(
        jnp.max(jnp.where(alive_mask, cached_scores, neg_fill), axis=-1),
        jnp.max(fresh_scores, axis=-1),
    )
    cached_weights = jnp.where(alive_mask, jnp.exp(cached_scores - peak_score[..., None]), 0.0)
    fresh_weights = jnp.exp(fresh_scores - peak_score[..., None])
    weight_sum = jnp.sum(cached_weights, axis=-1) + jnp.sum(fresh_weights, axis=-1)
    cached_probs = (cached_weights / weight_sum[..., None]).astype(jnp.bfloat16)
    fresh_probs = (fresh_weights / weight_sum[..., None]).astype(jnp.bfloat16)
    output = jnp.einsum(
        "rkgp,rpkd->rkgd", cached_probs, value_heads, preferred_element_type=jnp.float32
    )
    output = output + jnp.einsum(
        "rkgs,srkd->rkgd", fresh_probs, fresh_value_heads, preferred_element_type=jnp.float32
    )
    return output.astype(jnp.bfloat16).reshape(row_count, QH * HD)


def routing_tables(routes, route_weights, capacity):
    weight_sum = jnp.sum(route_weights, axis=1)
    experts = jnp.arange(WIN, dtype=jnp.int32)
    matches = routes[None, :, :] == experts[:, None, None]
    chosen = jnp.any(matches, axis=2)
    gate_share = (
        jnp.sum(jnp.where(matches, route_weights[None, :, :], 0.0), axis=2) / weight_sum[None, :]
    )
    slot_index = jnp.cumsum(chosen.astype(jnp.int32), axis=1) - 1
    places = jnp.arange(capacity, dtype=jnp.int32)
    picked = (slot_index[:, None, :] == places[None, :, None]) & chosen[:, None, :]
    return (picked.astype(jnp.bfloat16), picked.astype(jnp.float32) * gate_share[:, None, :])


def expert_rows(selected, gate_rows, up_rows, down_rows):
    gate_act = jnp.einsum("ecd,ehd->ech", selected, gate_rows, preferred_element_type=jnp.float32)
    up_act = jnp.einsum("ecd,ehd->ech", selected, up_rows, preferred_element_type=jnp.float32)
    product = (jax.nn.silu(gate_act) * up_act).astype(jnp.bfloat16)
    return jnp.einsum("ech,ehd->ecd", product, down_rows, preferred_element_type=jnp.float32)


def local_experts(selected, weighted, restored):
    outputs = expert_rows(selected, restored[0], restored[1], restored[2])
    return jnp.einsum("ecr,ecd->rd", weighted, outputs, precision=lax.Precision.HIGHEST)


def local(
    hidden_in,
    queries,
    key_cache,
    value_cache,
    new_keys,
    new_values,
    lengths,
    routes,
    route_weights,
    norm_gain,
    gate_master,
    up_master,
    down_master,
    out_proj,
):
    tp_count = lax.axis_size("tp")
    fsdp_pos = lax.axis_index("fsdp")
    tp_pos = lax.axis_index("tp")
    shard_rows = gate_master.shape[1]
    masters = jnp.stack([gate_master, up_master, down_master])
    owned_rows = (fsdp_pos * tp_count + tp_pos) * shard_rows + jnp.arange(
        shard_rows, dtype=jnp.int32
    )
    owner_map = owner_blocks(owned_rows)
    magnitude = jnp.max(jnp.abs(masters).reshape(3, WIN, shard_rows, D // BLOCK, BLOCK), axis=4)
    partial_max = jnp.max(
        jnp.where(owner_map[None, None, :, :, None], magnitude[:, :, :, None, :], 0.0), axis=2
    )
    block_max = lax.pmax(partial_max, ("fsdp", "tp"))
    scales = (block_max + epsilon) / fp_limit
    scale_log2 = jnp.log2(scales)
    local_factors = row_scales(scales, owner_map)
    tiles = masters.reshape(3, WIN, shard_rows, D // BLOCK, BLOCK)
    quantized = (
        grid_round(tiles / local_factors[..., None])
        .astype(jnp.bfloat16)
        .reshape(3, WIN, shard_rows, D)
    )
    gathered = lax.all_gather(quantized, "fsdp", axis=2, tiled=True)
    restored = dequantize(gathered, shard_rows, tp_count, tp_pos, scales)
    share_cols = D // tp_count
    own_start = tp_pos * share_cols
    current = lax.dynamic_slice_in_dim(hidden_in, own_start, share_cols, 1)
    for step_index in range(2):
        heads_local = attention_rows(
            queries[step_index],
            key_cache,
            value_cache,
            new_keys[: step_index + 1],
            new_values[: step_index + 1],
            lengths,
        )
        regrouped = lax.all_to_all(heads_local, "tp", split_axis=1, concat_axis=0, tiled=True)
        projected = jnp.dot(regrouped, out_proj, preferred_element_type=jnp.float32)
        mixed = (
            current.astype(jnp.float32) + sent_and_summed(projected.astype(jnp.bfloat16), "tp", 1)
        ).astype(jnp.bfloat16)
        values = mixed.astype(jnp.float32)
        squares = lax.psum(jnp.sum(values * values, axis=1), "tp")
        inverse = lax.rsqrt(squares / D + epsilon)
        own_gain = lax.dynamic_slice_in_dim(norm_gain, own_start, share_cols, 0)
        normed_share = (values * inverse[:, None] * own_gain[None, :]).astype(jnp.bfloat16)
        normed = collect(normed_share, "tp", 1)
        picked, weighted = routing_tables(routes[step_index], route_weights[step_index], CAP)
        selected = jnp.einsum(
            "ecr,rd->ecd", picked, normed, preferred_element_type=jnp.float32
        ).astype(jnp.bfloat16)
        partial_value = local_experts(selected, weighted, restored)
        current = (
            mixed.astype(jnp.float32) + sent_and_summed(partial_value.astype(jnp.bfloat16), "tp", 1)
        ).astype(jnp.bfloat16)
    return (current, scale_log2)


def solution(mesh):
    in_specs = (
        P("fsdp", None),
        P(None, ("fsdp", "tp"), None),
        P(("fsdp", "tp"), None, None),
        P(("fsdp", "tp"), None, None),
        P(None, ("fsdp", "tp"), None),
        P(None, ("fsdp", "tp"), None),
        P(("fsdp", "tp")),
        P(None, "fsdp", None),
        P(None, "fsdp", None),
        P(),
        P(None, ("fsdp", "tp"), None),
        P(None, ("fsdp", "tp"), None),
        P(None, ("fsdp", "tp"), None),
        P("tp", None),
    )
    out_specs = (P("fsdp", "tp"), P())
    return jax.shard_map(local, mesh=mesh, in_specs=in_specs, out_specs=out_specs, check_vma=False)
```

profile of v0, /device:TPU:0, one launch (start us, length us, event | category | flops | bytes accessed | tf_op | source)
XLA Modules:
  0.0 576.3 jit_solution(13156694128293218370)
XLA Ops:
  7.2 3.8 fusion.1
  11.3 0.3 select_reduce_fusion
  11.7 69.4 %pmax.7 = f32[3,8,12,32]{3,2,1,0:T(8,128)S(1)} all-reduce(f32[3,8,12,32]{3,2,1,0:T(8,128)S(1)} %copy.88), channel_id=1, replica_groups=mesh['fsdp'=16,'tp'=8] {'fsdp','tp'}, use_global_device_ids=true, to_apply=%region_11.12 | all-reduce | flops 9216 | bytes 73728 | tf_op jit(solution)/shard_map/pmax | solution.py:175
  81.1 0.3 convolution_bitcast_fusion.3
  81.3 0.2 copy.89
  81.6 7.7 %multiply_convert_fusion = bf16[3,8,12,4096]{3,1,2,0:T(8,128)(2,1)} fusion(f32[1,8,12,4096]{3,1,2,0:T(8,128)} %bitcast.173, f32[1,8,12,4096]{3,1,2,0:T(8,128)} %bitcast.175, f32[1,8,12,4096]{3,1,2,0:T(8,128)} %bitcast.177, f32[3,8,12,32]{1,3,2,0:T(8,128)S(1)} %copy.89), kind=kLoop, calls=%fused_computation.6 | loop fusion | flops 20054016 | bytes 7114752 | tf_op jit(solution)/shard_map/convert_element_type | solution.py:182
  89.8 0.8 select_reduce_fusion.2
  90.6 0.8 fusion.40
  91.4 0.5 fusion.31
  91.9 0.7 copy.83
  92.7 3.9 all-to-all-start
  96.9 0.3 fusion.41
  97.5 0.2 fusion.85
  97.7 0.5 convolution_bitcast_fusion.2
  98.3 2.0 fusion.28
  100.4 4.2 all-to-all-done
  104.6 5.2 convolution_convert_fusion.3
  109.8 0.9 copy.175
  110.7 3.5 all-to-all-start.1
  114.2 2.2 copy.90
  116.4 0.7 copy.98
  117.2 0.8 dynamic_slice.8
  117.9 7.5 %all-to-all-done.1 = bf16[8,64,512]{2,1,0:T(8,128)(2,1)S(1)} async-done(((bf16[8,64,512]{2,1,0:T(8,128)(2,1)}), bf16[8,64,512]{2,1,0:T(8,128)(2,1)S(1)}, u32[]{:S(2)}, u32[]{:S(2)}) %all-to-all-start.1) | async-done | bytes 524320 | tf_op jit(solution)/shard_map/all_to_all | solution.py:28
  125.5 3.4 all-to-all-start.4
  128.9 1.0 fusion.50
  129.9 24.9 %psum.14 = f32[64]{0:T(128)S(1)} all-reduce(f32[64]{0:T(128)S(1)} %get-tuple-element.16), channel_id=1, replica_groups=mesh['fsdp'=16,'tp'=8] {'tp'}, use_global_device_ids=true, to_apply=%region_8.9 | all-reduce | flops 64 | bytes 512 | tf_op jit(solution)/shard_map/psum | solution.py:205
  154.9 0.8 broadcast_in_dim.124
  155.8 3.5 all-to-all-start.2
  159.3 5.0 convolution_convert_fusion.1
  164.4 0.8 copy.173
  165.2 3.8 all-to-all-done.2
  169.0 3.9 all-to-all-start.5
  172.9 0.3 copy.85
  173.2 0.2 reshape.290
  173.5 0.3 convolution_convert_fusion.2
  173.8 122.2 %all-gather.2.cloned.1.call-done = bf16[3,8,192,4096]{3,1,2,0:T(8,128)(2,1)} async-done(((bf16[3,8,12,4096]{3,1,2,0:T(8,128)(2,1)}), bf16[3,8,192,4096]{3,1,2,0:T(8,128)(2,1)}) %all-gather.2.cloned.1.call-update) | async-done | bytes 37748752 | tf_op jit(solution)/shard_map/all_gather | solution.py:185
  296.0 36.6 %bitcast_convert_fusion = f32[3,8,192,32,128]{4,1,3,2,0:T(8,128)} fusion(bf16[3,8,192,4096]{3,1,2,0:T(8,128)(2,1)} %all-gather.2.cloned.1.call-done), kind=kLoop, calls=%fused_computation.2 | loop fusion | flops 18874368 | bytes 113246208 | tf_op jit(solution)/shard_map/reshape | solution.py:74
  332.7 38.8 %fusion = bf16[3,8,192,32,128]{4,3,2,1,0:T(8,128)(2,1)} fusion(f32[3,8,192,32,128]{4,1,3,2,0:T(8,128)} %bitcast_convert_fusion, f32[3,8,192,32]{3,2,1,0:T(8,128)} %copy.90), kind=kLoop, calls=%fused_computation.1 | loop fusion | flops 37748736 | bytes 113836032 | tf_op jit(solution)/shard_map/convert_element_type | solution.py:75
  371.5 25.3 %fusion.120 = (bf16[1,8,192,32,128]{4,3,2,1,0:T(8,128)(2,1)}, bf16[1,8,192,32,128]{4,3,2,1,0:T(8,128)(2,1)}, bf16[1,8,192,32,128]{4,3,2,1,0:T(8,128)(2,1)}) fusion(bf16[3,8,192,32,128]{4,3,2,1,0:T(8,128)(2,1)} %fusion), kind=kLoop, calls=%fused_computation.189 | loop fusion | bytes 75497472 | tf_op jit(solution)/shard_map/slice | solution.py:142
  396.8 19.3 %squeeze.16 = bf16[8,192,4096]{2,1,0:T(8,128)(2,1)} reshape(bf16[1,8,192,32,128]{4,3,2,1,0:T(8,128)(2,1)} %get-tuple-element.19) | data formatting | bytes 25165824 | tf_op jit(solution)/shard_map/squeeze | solution.py:142
  416.1 19.3 %squeeze.7 = bf16[8,192,4096]{2,1,0:T(8,128)(2,1)} reshape(bf16[1,8,192,32,128]{4,3,2,1,0:T(8,128)(2,1)} %get-tuple-element.20) | data formatting | bytes 25165824 | tf_op jit(solution)/shard_map/squeeze | solution.py:142
  435.4 19.3 %squeeze.6 = bf16[8,192,4096]{2,1,0:T(8,128)(2,1)} reshape(bf16[1,8,192,32,128]{4,3,2,1,0:T(8,128)(2,1)} %get-tuple-element.18) | data formatting | bytes 25165824 | tf_op jit(solution)/shard_map/squeeze | solution.py:142
  454.7 7.9 %fusion.122 = f32[8,8,192]{2,1,0:T(8,128)S(1)} fusion(bf16[8,8,4096]{2,1,0:T(8,128)(2,1)S(1)} %convolution_convert_fusion.2, bf16[8,192,4096]{2,1,0:T(8,128)(2,1)} %squeeze.6), kind=kOutput, calls=%fused_computation.191 | convolution fusion | flops 100663296 | bytes 13156352 | tf_op jit(solution)/shard_map/ecd,ehd->ech/dot_general | solution.py:135
  462.6 10.7 %fusion.39 = f32[8,8,4096]{2,1,0:T(8,128)S(1)} fusion(bf16[8,192,4096]{2,1,0:T(8,128)(2,1)} %squeeze.16, bf16[8,8,4096]{2,1,0:T(8,128)(2,1)S(1)} %convolution_convert_fusion.2, bf16[8,192,4096]{2,1,0:T(8,128)(2,1)} %squeeze.7, f32[8,8,192]{2,1,0:T(8,128)S(1)} %fusion.122), kind=kOutput, calls=%fused_computation.48 | convolution fusion | flops 201400320 | bytes 26787840 | tf_op jit(solution)/shard_map/ech,ehd->ecd/dot_general | solution.py:138
  473.3 1.6 fusion.2
  474.9 0.9 copy.174
  475.8 6.4 %all-to-all-start.3 = ((bf16[8,64,512]{2,1,0:T(8,128)(2,1)}), bf16[8,64,512]{2,1,0:T(8,128)(2,1)S(1)}, u32[]{:S(2)}, u32[]{:S(2)}) async-start(bf16[8,64,512]{2,1,0:T(8,128)(2,1)} %bitcast.169), calls=%async_computation.3 | async-start | bytes 1048576 | tf_op jit(solution)/shard_map/all_to_all | solution.py:28
  482.2 0.2 reduce_window_sum.18
  482.5 11.0 %all-to-all-done.3 = bf16[8,64,512]{2,1,0:T(8,128)(2,1)S(1)} async-done(((bf16[8,64,512]{2,1,0:T(8,128)(2,1)}), bf16[8,64,512]{2,1,0:T(8,128)(2,1)S(1)}, u32[]{:S(2)}, u32[]{:S(2)}) %all-to-all-start.3) | async-done | bytes 524320 | tf_op jit(solution)/shard_map/all_to_all | solution.py:28
  493.7 21.1 %psum.15 = f32[64]{0:T(128)S(1)} all-reduce(f32[64]{0:T(128)S(1)} %get-tuple-element.14), channel_id=1, replica_groups=mesh['fsdp'=16,'tp'=8] {'tp'}, use_global_device_ids=true, to_apply=%region_23.24 | all-reduce | flops 64 | bytes 512 | tf_op jit(solution)/shard_map/psum | solution.py:205
  514.9 0.9 broadcast_in_dim.130
  515.8 3.7 all-to-all-start.6
  519.6 9.3 %all-to-all-done.6 = bf16[8,64,512]{2,1,0:T(8,128)(2,1)S(1)} async-done(((bf16[8,64,512]{2,1,0:T(8,128)(2,1)}), bf16[8,64,512]{2,1,0:T(8,128)(2,1)S(1)}, u32[]{:S(2)}, u32[]{:S(2)}) %all-to-all-start.6) | async-done | bytes 524320 | tf_op jit(solution)/shard_map/all_to_all | solution.py:34
  528.9 0.3 copy.100
  529.2 0.2 reshape.294
  529.4 0.3 convolution_convert_fusion
  529.7 7.9 %fusion.123 = f32[8,8,192]{2,1,0:T(8,128)S(1)} fusion(bf16[8,8,4096]{2,1,0:T(8,128)(2,1)S(1)} %convolution_convert_fusion, bf16[8,192,4096]{2,1,0:T(8,128)(2,1)} %squeeze.6), kind=kOutput, calls=%fused_computation.192 | convolution fusion | flops 100663296 | bytes 13156352 | tf_op jit(solution)/shard_map/ecd,ehd->ech/dot_general | solution.py:135
  537.7 14.4 %fusion.38 = f32[8,8,4096]{2,1,0:T(8,128)} fusion(bf16[8,192,4096]{2,1,0:T(8,128)(2,1)} %squeeze.16, bf16[8,8,4096]{2,1,0:T(8,128)(2,1)S(1)} %convolution_convert_fusion, bf16[8,192,4096]{2,1,0:T(8,128)(2,1)} %squeeze.7, f32[8,8,192]{2,1,0:T(8,128)S(1)} %fusion.123), kind=kOutput, calls=%fused_computation.47 | convolution fusion | flops 201400320 | bytes 26787840 | tf_op jit(solution)/shard_map/ech,ehd->ecd/dot_general | solution.py:138
  552.0 2.8 fusion.3
  554.8 0.8 copy.172
  555.7 3.5 all-to-all-start.7
  559.2 0.7 copy.104
  559.9 8.8 %all-to-all-done.7 = bf16[8,64,512]{2,1,0:T(8,128)(2,1)S(1)} async-done(((bf16[8,64,512]{2,1,0:T(8,128)(2,1)}), bf16[8,64,512]{2,1,0:T(8,128)(2,1)S(1)}, u32[]{:S(2)}, u32[]{:S(2)}) %all-to-all-start.7) | async-done | bytes 524320 | tf_op jit(solution)/shard_map/all_to_all | solution.py:28
  568.8 0.6 fusion.57
  (67 shorter events, 2.2 us)
Async XLA Ops:
  7.2 82.6 %copy-start = (bf16[8,256,512]{2,1,0:T(8,128)(2,1)S(1)}, bf16[8,256,512]{2,1,0:T(8,128)(2,1)}, u32[]{:S(2)}) copy-start(bf16[8,256,512]{2,1,0:T(8,128)(2,1)} %param.16) | copy-start | bytes 6291460
  7.2 288.8 %all-gather.2.cloned.1.call-start = ((), (), s32[]{:S(2)}) async-start(), calls=%async_computation.8 | async-start | bytes 40108032 | tf_op jit(solution)/shard_map/all_gather | solution.py:185
  81.6 7.8 %copy-start.2 = (bf16[2,8,8192]{2,1,0:T(8,128)(2,1)S(1)}, bf16[2,8,8192]{2,1,0:T(8,128)(2,1)}, u32[]{:S(2)}) copy-start(bf16[2,8,8192]{2,1,0:T(8,128)(2,1)} %param.15) | copy-start | bytes 786436
  81.6 7.9 %copy-start.5 = (bf16[2,8,512]{2,1,0:T(8,128)(2,1)S(1)}, bf16[2,8,512]{2,1,0:T(8,128)(2,1)}, u32[]{:S(2)}) copy-start(bf16[2,8,512]{2,1,0:T(8,128)(2,1)} %param.19) | copy-start | bytes 49156
  81.6 7.9 %copy-start.7 = (s32[8]{0:T(128)S(1)}, s32[8]{0:T(128)}, u32[]{:S(2)}) copy-start(s32[8]{0:T(128)} %param.20) | copy-start | bytes 100
  81.6 8.0 %copy-start.6 = (bf16[2,8,512]{2,1,0:T(8,128)(2,1)S(1)}, bf16[2,8,512]{2,1,0:T(8,128)(2,1)}, u32[]{:S(2)}) copy-start(bf16[2,8,512]{2,1,0:T(8,128)(2,1)} %param.18) | copy-start | bytes 49156
  89.4 2.0 copy-start.8
  90.5 6.0 %copy-start.3 = (s32[2,64,8]{1,2,0:T(8,128)S(1)}, s32[2,64,8]{1,2,0:T(8,128)}, u32[]{:S(2)}) copy-start(s32[2,64,8]{1,2,0:T(8,128)} %param.21) | copy-start | bytes 12292
  91.9 8.5 %copy-start.4 = (f32[2,64,8]{1,2,0:T(8,128)S(1)}, f32[2,64,8]{1,2,0:T(8,128)}, u32[]{:S(2)}) copy-start(f32[2,64,8]{1,2,0:T(8,128)} %param.22) | copy-start | bytes 12292
  92.7 11.9 %all-to-all-start = ((bf16[8,8,1024]{2,0,1:T(8,128)(2,1)}), bf16[8,8,1024]{2,0,1:T(8,128)(2,1)S(1)}, u32[]{:S(2)}, u32[]{:S(2)}) async-start(bf16[8,8,1024]{2,0,1:T(8,128)(2,1)} %copy.83), calls=%async_computation | async-start | bytes 262144 | tf_op jit(solution)/shard_map/all_to_all | solution.py:199
  110.7 14.8 %all-to-all-start.1 = ((bf16[8,64,512]{2,1,0:T(8,128)(2,1)}), bf16[8,64,512]{2,1,0:T(8,128)(2,1)S(1)}, u32[]{:S(2)}, u32[]{:S(2)}) async-start(bf16[8,64,512]{2,1,0:T(8,128)(2,1)} %bitcast.171), calls=%async_computation.1 | async-start | bytes 1048576 | tf_op jit(solution)/shard_map/all_to_all | solution.py:28
  125.5 29.5 %all-to-all-start.4 = ((bf16[8,8,1024]{2,0,1:T(8,128)(2,1)}), bf16[8,8,1024]{2,0,1:T(8,128)(2,1)S(1)}, u32[]{:S(2)}, u32[]{:S(2)}) async-start(bf16[8,8,1024]{2,0,1:T(8,128)(2,1)} %copy.98), calls=%async_computation.4 | async-start | bytes 262144 | tf_op jit(solution)/shard_map/all_to_all | solution.py:199
  155.8 13.2 %all-to-all-start.2 = ((bf16[8,64,512]{2,1,0:T(8,128)(2,1)}), bf16[8,64,512]{2,1,0:T(8,128)(2,1)S(1)}, u32[]{:S(2)}, u32[]{:S(2)}) async-start(bf16[8,64,512]{2,1,0:T(8,128)(2,1)} %broadcast_in_dim.124), calls=%async_computation.2 | async-start | bytes 1048576 | tf_op jit(solution)/shard_map/all_to_all | solution.py:34
  169.0 306.8 %all-to-all-start.5 = ((bf16[8,64,512]{2,1,0:T(8,128)(2,1)}), bf16[8,64,512]{2,1,0:T(8,128)(2,1)S(1)}, u32[]{:S(2)}, u32[]{:S(2)}) async-start(bf16[8,64,512]{2,1,0:T(8,128)(2,1)} %bitcast.167), calls=%async_computation.5 | async-start | bytes 1048576 | tf_op jit(solution)/shard_map/all_to_all | solution.py:28
  475.8 17.7 %all-to-all-start.3 = ((bf16[8,64,512]{2,1,0:T(8,128)(2,1)}), bf16[8,64,512]{2,1,0:T(8,128)(2,1)S(1)}, u32[]{:S(2)}, u32[]{:S(2)}) async-start(bf16[8,64,512]{2,1,0:T(8,128)(2,1)} %bitcast.169), calls=%async_computation.3 | async-start | bytes 1048576 | tf_op jit(solution)/shard_map/all_to_all | solution.py:28
  515.8 13.1 %all-to-all-start.6 = ((bf16[8,64,512]{2,1,0:T(8,128)(2,1)}), bf16[8,64,512]{2,1,0:T(8,128)(2,1)S(1)}, u32[]{:S(2)}, u32[]{:S(2)}) async-start(bf16[8,64,512]{2,1,0:T(8,128)(2,1)} %broadcast_in_dim.130), calls=%async_computation.6 | async-start | bytes 1048576 | tf_op jit(solution)/shard_map/all_to_all | solution.py:34
  537.6 31.8 %copy-start.1 = (bf16[8,256,512]{2,1,0:T(8,128)(2,1)S(1)}, bf16[8,256,512]{2,1,0:T(8,128)(2,1)}, u32[]{:S(2)}) copy-start(bf16[8,256,512]{2,1,0:T(8,128)(2,1)} %param.16) | copy-start | bytes 6291460
  555.7 13.1 %all-to-all-start.7 = ((bf16[8,64,512]{2,1,0:T(8,128)(2,1)}), bf16[8,64,512]{2,1,0:T(8,128)(2,1)S(1)}, u32[]{:S(2)}, u32[]{:S(2)}) async-start(bf16[8,64,512]{2,1,0:T(8,128)(2,1)} %bitcast.165), calls=%async_computation.7 | async-start | bytes 1048576 | tf_op jit(solution)/shard_map/all_to_all | solution.py:28
Sparse Core Ops, SparseCore 0:
  89.5 206.4 all-gather.1
where the time goes:
time: 579 us; the launch traced here: 576 us
  waiting for transfers between devices  167 us (29%)
  blocking collectives  115 us (20%)
  local copies, waits for them, and re-layouts  95.3 us (16%)
  other arithmetic  90.6 us (16%)
  matrix products  61.6 us (11%)
  starting transfers between devices  31.9 us (6%)
  between operations  14.5 us (3%)
    all_gather x1, waiting for transfers between devices, local(): gathered = lax.all_gather(quantized, 'fsdp', axis=2, tiled=True)  122 us
    pmax x1, blocking collectives, local(): block_max = lax.pmax(partial_max, ('fsdp', 'tp'))  69.4 us
    squeeze x3, local copies, waits for them, and re-layouts, local_experts(): outputs = expert_rows(selected, restored[0], restored[1], restored[2])  57.9 us
    psum x2, blocking collectives, local(): squares = lax.psum(jnp.sum(values * values, axis=1), 'tp')  46.1 us
    convert_element_type x1, other arithmetic, dequantize(): (tiles * factors[..., None]).astype(jnp.bfloat16).reshape(3, WIN, count, D)  38.8 us
    reshape x1, other arithmetic, dequantize(): shard_piece.astype(jnp.float32).reshape(3, WIN, count, D // BLOCK, BLOCK)  36.6 us
    all_to_all x4, waiting for transfers between devices, sent_and_summed(): lax.all_to_all(blocks, axis, split_axis=0, concat_axis=0, tiled=True)  27.3 us
    slice x1, local copies, waits for them, and re-layouts, local_experts(): outputs = expert_rows(selected, restored[0], restored[1], restored[2])  25.3 us
  transfers between devices with their start and end apart: 9, of which 7 were waited for; matrix products, arithmetic and copies ran while one was open for 36% of the time, Pallas kernels for 0%

commit v1 on v0

--- a/solution.py
+++ b/solution.py
@@ -182,7 +182,9 @@
         .astype(jnp.bfloat16)
         .reshape(3, WIN, shard_rows, D)
     )
-    gathered = lax.all_gather(quantized, "fsdp", axis=2, tiled=True)
+    gathered = jnp.concatenate(
+        lax.all_to_all(jnp.stack([quantized] * lax.axis_size("fsdp")), "fsdp", 0, 0), axis=2
+    )
     restored = dequantize(gathered, shard_rows, tp_count, tp_pos, scales)
     share_cols = D // tp_count
     own_start = tp_pos * share_cols

time: 579 us -> 1180 us (2.04)
  waiting for transfers between devices: 167 us -> 613 us
  local copies, waits for them, and re-layouts: 95.3 us -> 211 us
  matrix products: 61.6 us -> 98.8 us
  between operations: 14.5 us -> 1.8 us
  starting transfers between devices: 31.9 us -> 43.7 us
    all_to_all x0 -> x1, waiting for transfers between devices: none -> 579 us  [local(): lax.all_to_all(jnp.stack([quantized] * lax.axis_size('fsdp')), 'fsdp', 0, 0)]
    all_gather x1 -> x0, waiting for transfers between devices: 122 us -> none  [local(): gathered = lax.all_gather(quantized, 'fsdp', axis=2, tiled=True)]
    unnamed x22 -> x65, local copies, waits for them, and re-layouts: 0.82 us -> 51.6 us
    convert_element_type x0 -> x1, local copies, waits for them, and re-layouts: none -> 50.2 us  [dequantize(): shard_piece.astype(jnp.float32).reshape(3, WIN, count, D // BLOCK, BLOCK)]
    reshape x1 -> x0, other arithmetic: 36.6 us -> none  [dequantize(): shard_piece.astype(jnp.float32).reshape(3, WIN, count, D // BLOCK, BLOCK)]
    convert_element_type x0 -> x1, other arithmetic: none -> 36.6 us  [dequantize(): shard_piece.astype(jnp.float32).reshape(3, WIN, count, D // BLOCK, BLOCK)]
    dot_general x0 -> x2, matrix products: none -> 26.5 us  [expert_rows(): jnp.einsum('ecd,ehd->ech', selected, up_rows, preferred_element_type=jnp....]
    another operation x1 -> x2, local copies, waits for them, and re-layouts: 0.01 us -> 13.6 us  [the longest x1 13.5 us: local(): jnp.stack([quantized] * lax.axis_size('fsdp'))]
  transfers between devices with their start and end apart: 9 -> 9, of which waited for: 7 -> 6; matrix products, arithmetic and copies ran while one was open for 36% -> 28% of each run, Pallas kernels for 0% -> 0%
where the time goes in v1:
time: 1180 us; the launch traced here: 1170 us
  waiting for transfers between devices  613 us (52%)
  local copies, waits for them, and re-layouts  211 us (18%)
  blocking collectives  114 us (10%)
  matrix products  98.8 us (8%)
  other arithmetic  92.4 us (8%)
  starting transfers between devices  43.7 us (4%)
    all_to_all x1, waiting for transfers between devices, local(): lax.all_to_all(jnp.stack([quantized] * lax.axis_size('fsdp')), 'fsdp', 0, 0)  579 us
    pmax x1, blocking collectives, local(): block_max = lax.pmax(partial_max, ('fsdp', 'tp'))  68.2 us
    squeeze x3, local copies, waits for them, and re-layouts, local_experts(): outputs = expert_rows(selected, restored[0], restored[1], restored[2])  58 us
    unnamed x65, local copies, waits for them, and re-layouts  51.6 us
    convert_element_type x1, local copies, waits for them, and re-layouts, dequantize(): shard_piece.astype(jnp.float32).reshape(3, WIN, count, D // BLOCK, BLOCK)  50.2 us
    psum x2, blocking collectives, local(): squares = lax.psum(jnp.sum(values * values, axis=1), 'tp')  45.7 us
    convert_element_type x1, other arithmetic, dequantize(): (tiles * factors[..., None]).astype(jnp.bfloat16).reshape(3, WIN, count, D)  37.9 us
    convert_element_type x1, other arithmetic, dequantize(): shard_piece.astype(jnp.float32).reshape(3, WIN, count, D // BLOCK, BLOCK)  36.6 us
  transfers between devices with their start and end apart: 9, of which 6 were waited for; matrix products, arithmetic and copies ran while one was open for 28% of the time, Pallas kernels for 0%

profile of v1, /device:TPU:0, one launch (start us, length us, event | category | flops | bytes accessed | tf_op | source)
XLA Modules:
  0.0 1174.5 jit_solution(4109676590047936161)
XLA Ops:
  0.7 1.1 slice_bitcast_fusion.1
  1.8 0.9 iota_compare_fusion.6
  2.8 0.7 slice_bitcast_fusion.2
  3.7 0.8 select_reduce_fusion.2
  4.4 0.8 fusion.59
  5.9 0.7 copy.86
  6.6 7.0 all-to-all-start
  14.5 2.0 fusion.39
  16.6 4.9 all-to-all-done
  21.5 4.9 convolution_convert_fusion.3
  26.5 0.8 copy.202
  27.3 3.5 all-to-all-start.1
  30.8 3.2 fusion.12
  34.1 0.7 copy.104
  35.3 68.2 %pmax.7 = f32[3,8,12,32]{3,2,1,0:T(8,128)S(1)} all-reduce(f32[3,8,12,32]{3,2,1,0:T(8,128)S(1)} %copy.91), channel_id=1, replica_groups=mesh['fsdp'=16,'tp'=8] {'fsdp','tp'}, use_global_device_ids=true, to_apply=%region_11.12 | all-reduce | flops 9216 | bytes 73728 | tf_op jit(solution)/shard_map/pmax | solution.py:175
  104.1 0.8 dynamic_slice.8
  104.8 4.1 all-to-all-start.5
  109.0 1.0 fusion.69
  110.0 24.6 %psum.14 = f32[64]{0:T(128)S(1)} all-reduce(f32[64]{0:T(128)S(1)} %get-tuple-element.16), channel_id=1, replica_groups=mesh['fsdp'=16,'tp'=8] {'tp'}, use_global_device_ids=true, to_apply=%region_8.9 | all-reduce | flops 64 | bytes 512 | tf_op jit(solution)/shard_map/psum | solution.py:207
  134.7 0.8 broadcast_in_dim.124
  135.6 3.5 all-to-all-start.2
  139.1 7.4 multiply_convert_fusion.1
  146.5 2.2 all-to-all-done.2
  148.7 13.5 %stack.31 = bf16[16,3,8,12,4096]{4,2,3,1,0:T(8,128)(2,1)} broadcast(bf16[3,8,12,4096]{3,1,2,0:T(8,128)(2,1)} %multiply_convert_fusion.1), dimensions={1,2,3,4} | broadcast | bytes 40108032 | tf_op jit(solution)/shard_map/stack | solution.py:186
  162.2 6.4 all-to-all-start.3
  169.0 0.5 convolution_bitcast_fusion.2
  169.5 2.1 copy.94
  171.7 0.6 slice_reduce_fusion
  172.2 0.6 select_reduce_fusion.3
  172.8 0.6 broadcast_divide_fusion.1
  173.5 5.0 convolution_convert_fusion.1
  178.4 0.9 copy.200
  179.8 1.1 convolution_convert_fusion.2
  180.9 578.7 %all-to-all-done.3 = bf16[16,3,8,12,4096]{4,2,3,1,0:T(8,128)(2,1)} async-done(((bf16[16,3,8,12,4096]{4,2,3,1,0:T(8,128)(2,1)}), bf16[16,3,8,12,4096]{4,2,3,1,0:T(8,128)(2,1)}, u32[]{:S(2)}, u32[]{:S(2)}) %all-to-all-start.3) | async-done | bytes 37748768 | tf_op jit(solution)/shard_map/all_to_all | solution.py:186
  759.6 4.9 all-to-all-start.6
  764.5 36.6 %convert_bitcast_fusion = f32[3,8,16,12,4096]{4,1,3,0,2:T(8,128)} fusion(bf16[16,3,8,12,4096]{4,2,3,1,0:T(8,128)(2,1)} %all-to-all-done.3), kind=kLoop, calls=%fused_computation | loop fusion | flops 18874368 | bytes 113246208 | tf_op jit(solution)/shard_map/convert_element_type | solution.py:74
  801.1 50.2 %copy.93 = f32[3,8,16,12,4096]{4,1,3,2,0:T(8,128)} copy(f32[3,8,16,12,4096]{4,1,3,0,2:T(8,128)} %convert_bitcast_fusion) | data formatting | bytes 150994944 | tf_op jit(solution)/shard_map/convert_element_type | solution.py:74
  851.3 49.6 %copy.125 = f32[576,8,32,128]{3,2,1,0:T(8,128)} copy(f32[576,8,32,128]{3,1,2,0:T(8,128)} %bitcast.63) | data formatting | bytes 150994944
  900.9 37.9 %multiply_convert_fusion = bf16[3,8,192,32,128]{4,3,1,2,0:T(8,128)(2,1)} fusion(f32[3,8,192,32,128]{4,3,1,2,0:T(8,128)} %bitcast.66, f32[3,8,192,32]{3,1,2,0:T(8,128)} %copy.94), kind=kLoop, calls=%fused_computation.1 | loop fusion | flops 37748736 | bytes 113836032 | tf_op jit(solution)/shard_map/convert_element_type | solution.py:75
  938.8 25.8 %fusion.125 = (bf16[1,8,192,32,128]{4,3,1,2,0:T(8,128)(2,1)}, bf16[1,8,192,32,128]{4,3,1,2,0:T(8,128)(2,1)}, bf16[1,8,192,32,128]{4,3,1,2,0:T(8,128)(2,1)}) fusion(bf16[3,8,192,32,128]{4,3,1,2,0:T(8,128)(2,1)} %multiply_convert_fusion), kind=kLoop, calls=%fused_computation.184 | loop fusion | bytes 75497472 | tf_op jit(solution)/shard_map/slice | solution.py:142
  964.5 19.3 %reshape.302 = bf16[8,192,4096]{2,0,1:T(8,128)(2,1)} reshape(bf16[1,8,192,32,128]{4,3,1,2,0:T(8,128)(2,1)} %get-tuple-element.19) | data formatting | bytes 25165824 | tf_op jit(solution)/shard_map/squeeze | solution.py:142
  983.8 19.3 %reshape.301 = bf16[8,192,4096]{2,0,1:T(8,128)(2,1)} reshape(bf16[1,8,192,32,128]{4,3,1,2,0:T(8,128)(2,1)} %get-tuple-element.20) | data formatting | bytes 25165824 | tf_op jit(solution)/shard_map/squeeze | solution.py:142
  1003.1 19.4 %reshape.303 = bf16[8,192,4096]{2,0,1:T(8,128)(2,1)} reshape(bf16[1,8,192,32,128]{4,3,1,2,0:T(8,128)(2,1)} %get-tuple-element.18) | data formatting | bytes 25165824 | tf_op jit(solution)/shard_map/squeeze | solution.py:142
  1022.5 12.9 %fusion.10 = f32[8,8,192]{2,1,0:T(8,128)S(1)} fusion(bf16[8,8,4096]{2,1,0:T(8,128)(2,1)S(1)} %copy-done.3, bf16[8,192,4096]{2,0,1:T(8,128)(2,1)} %reshape.301), kind=kOutput, calls=%fused_computation.12 | convolution fusion | flops 100663296 | bytes 13156352 | tf_op jit(solution)/shard_map/ecd,ehd->ech/dot_general | solution.py:135
  1035.4 13.4 %fusion.48 = bf16[8,8,192]{2,1,0:T(8,128)(2,1)S(1)} fusion(bf16[8,8,4096]{2,1,0:T(8,128)(2,1)S(1)} %copy-done.3, bf16[8,192,4096]{2,0,1:T(8,128)(2,1)} %reshape.302, f32[8,8,192]{2,1,0:T(8,128)S(1)} %fusion.10), kind=kOutput, calls=%fused_computation.48 | convolution fusion | flops 100737024 | bytes 13180928 | tf_op jit(solution)/shard_map/ecd,ehd->ech/dot_general | solution.py:136
  1048.8 13.3 %fusion.2 = f32[8,8,4096]{2,1,0:T(8,128)S(1)} fusion(bf16[8,8,192]{2,1,0:T(8,128)(2,1)S(1)} %fusion.48, bf16[8,192,4096]{2,0,1:T(8,128)(2,1)S(1)} %bitcast.181), kind=kOutput, calls=%fused_computation.4 | convolution fusion | flops 100663296 | bytes 13656064 | tf_op jit(solution)/shard_map/ech,ehd->ecd/dot_general | solution.py:138
  1062.2 1.6 fusion.13
  1063.8 0.9 copy.201
  1064.6 7.2 all-to-all-start.4
  1072.1 1.1 convert_reduce_fusion.1
  1073.2 8.9 all-to-all-done.4
  1082.3 21.2 %psum.15 = f32[64]{0:T(128)S(1)} all-reduce(f32[64]{0:T(128)S(1)} %get-tuple-element.14), channel_id=1, replica_groups=mesh['fsdp'=16,'tp'=8] {'tp'}, use_global_device_ids=true, to_apply=%region_23.24 | all-reduce | flops 64 | bytes 512 | tf_op jit(solution)/shard_map/psum | solution.py:207
  1103.6 0.9 broadcast_in_dim.130
  1104.5 3.5 all-to-all-start.7
  1108.0 9.5 all-to-all-done.7
  1118.4 12.9 %fusion.8 = f32[8,8,192]{2,1,0:T(8,128)S(1)} fusion(bf16[8,8,4096]{2,1,0:T(8,128)(2,1)S(1)} %convolution_convert_fusion, bf16[8,192,4096]{2,0,1:T(8,128)(2,1)} %reshape.301), kind=kOutput, calls=%fused_computation.10 | convolution fusion | flops 100663296 | bytes 13156352 | tf_op jit(solution)/shard_map/ecd,ehd->ech/dot_general | solution.py:135
  1131.3 13.1 %fusion.54 = bf16[8,8,192]{2,1,0:T(8,128)(2,1)S(1)} fusion(bf16[8,8,4096]{2,1,0:T(8,128)(2,1)S(1)} %convolution_convert_fusion, bf16[8,192,4096]{2,0,1:T(8,128)(2,1)} %reshape.302, f32[8,8,192]{2,1,0:T(8,128)S(1)} %fusion.8), kind=kOutput, calls=%fused_computation.50 | convolution fusion | flops 100737024 | bytes 13180928 | tf_op jit(solution)/shard_map/ecd,ehd->ech/dot_general | solution.py:136
  1144.5 13.4 %fusion = f32[8,8,4096]{2,1,0:T(8,128)S(1)} fusion(bf16[8,8,192]{2,1,0:T(8,128)(2,1)S(1)} %fusion.54, bf16[8,192,4096]{2,0,1:T(8,128)(2,1)S(1)} %bitcast.183), kind=kOutput, calls=%fused_computation.2 | convolution fusion | flops 100663296 | bytes 13656064 | tf_op jit(solution)/shard_map/ech,ehd->ecd/dot_general | solution.py:138
  1157.9 1.6 fusion.14
  1159.5 0.8 copy.199
  1160.3 3.5 all-to-all-start.8
  1163.9 0.7 copy.110
  1164.6 8.8 all-to-all-done.8
  1173.5 0.6 fusion.76
  (115 shorter events, 5.4 us)
Async XLA Ops:
  0.6 3.0 copy-start
  0.6 4.6 copy-start.20
  0.7 4.6 copy-start.23
  4.4 9.2 copy-start.21
  6.6 14.9 %all-to-all-start = ((bf16[8,8,1024]{2,0,1:T(8,128)(2,1)}), bf16[8,8,1024]{2,0,1:T(8,128)(2,1)S(1)}, u32[]{:S(2)}, u32[]{:S(2)}) async-start(bf16[8,8,1024]{2,0,1:T(8,128)(2,1)} %copy.86), calls=%async_computation | async-start | bytes 262144 | tf_op jit(solution)/shard_map/all_to_all | solution.py:201
  16.6 14.2 %copy-start.2 = (f32[8,12,4096]{2,0,1:T(8,128)S(1)}, f32[8,12,4096]{2,0,1:T(8,128)}, u32[]{:S(2)}) copy-start(f32[8,12,4096]{2,0,1:T(8,128)} %param.26) | copy-start | bytes 4718596
  27.3 77.5 %all-to-all-start.1 = ((bf16[8,64,512]{2,1,0:T(8,128)(2,1)}), bf16[8,64,512]{2,1,0:T(8,128)(2,1)S(1)}, u32[]{:S(2)}, u32[]{:S(2)}) async-start(bf16[8,64,512]{2,1,0:T(8,128)(2,1)} %bitcast.179), calls=%async_computation.1 | async-start | bytes 1048576 | tf_op jit(solution)/shard_map/all_to_all | solution.py:28
  103.5 65.5 %copy-start.4 = (f32[3,8,12,32]{3,2,1,0:T(8,128)}, f32[3,8,12,32]{3,2,1,0:T(8,128)S(1)}, u32[]{:S(2)}) copy-start(f32[3,8,12,32]{3,2,1,0:T(8,128)S(1)} %pmax.7) | copy-start | bytes 110596
  104.8 41.6 %copy-start.12 = (f32[512]{0:T(512)}, f32[512]{0:T(512)S(1)}, u32[]{:S(2)}) copy-start(f32[512]{0:T(512)S(1)} %dynamic_slice.8) | copy-start | bytes 6148
  104.8 29.9 %all-to-all-start.5 = ((bf16[8,8,1024]{2,0,1:T(8,128)(2,1)}), bf16[8,8,1024]{2,0,1:T(8,128)(2,1)S(1)}, u32[]{:S(2)}, u32[]{:S(2)}) async-start(bf16[8,8,1024]{2,0,1:T(8,128)(2,1)} %copy.104), calls=%async_computation.5 | async-start | bytes 262144 | tf_op jit(solution)/shard_map/all_to_all | solution.py:201
  110.0 36.4 %copy-start.6 = (bf16[64,512]{1,0:T(8,128)(2,1)}, bf16[64,512]{1,0:T(8,128)(2,1)S(1)}, u32[]{:S(2)}) copy-start(bf16[64,512]{1,0:T(8,128)(2,1)S(1)} %get-tuple-element.17) | copy-start | bytes 196612
  135.6 13.1 %all-to-all-start.2 = ((bf16[8,64,512]{2,1,0:T(8,128)(2,1)}), bf16[8,64,512]{2,1,0:T(8,128)(2,1)S(1)}, u32[]{:S(2)}, u32[]{:S(2)}) async-start(bf16[8,64,512]{2,1,0:T(8,128)(2,1)} %broadcast_in_dim.124), calls=%async_computation.2 | async-start | bytes 1048576 | tf_op jit(solution)/shard_map/all_to_all | solution.py:34
  162.2 6.5 copy-start.18
  162.2 9.5 copy-start.19
  162.2 597.4 %all-to-all-start.3 = ((bf16[16,3,8,12,4096]{4,2,3,1,0:T(8,128)(2,1)}), bf16[16,3,8,12,4096]{4,2,3,1,0:T(8,128)(2,1)}, u32[]{:S(2)}, u32[]{:S(2)}) async-start(bf16[16,3,8,12,4096]{4,2,3,1,0:T(8,128)(2,1)} %stack.31), calls=%async_computation.3 | async-start | bytes 75497472 | tf_op jit(solution)/shard_map/all_to_all | solution.py:186
  168.7 3.5 copy-start.10
  168.7 9.7 copy-start.16
  172.8 5.6 copy-start.8
  759.6 305.0 %all-to-all-start.6 = ((bf16[8,64,512]{2,1,0:T(8,128)(2,1)}), bf16[8,64,512]{2,1,0:T(8,128)(2,1)}, u32[]{:S(2)}, u32[]{:S(2)}) async-start(bf16[8,64,512]{2,1,0:T(8,128)(2,1)} %bitcast.175), calls=%async_computation.6 | async-start | bytes 1048576 | tf_op jit(solution)/shard_map/all_to_all | solution.py:28
  1003.1 19.4 %copy-start.3 = (bf16[8,8,4096]{2,1,0:T(8,128)(2,1)S(1)}, bf16[8,8,4096]{2,1,0:T(8,128)(2,1)}, u32[]{:S(2)}) copy-start(bf16[8,8,4096]{2,1,0:T(8,128)(2,1)} %convolution_convert_fusion.2) | copy-start | bytes 1572868
  1022.5 26.3 %slice-start = ((s8[12582912]{0:T(1024)(128)(4,1)}), s8[4194304]{0:T(1024)(128)(4,1)S(1)}, s32[]{:S(2)}) async-start(s8[12582912]{0:T(1024)(128)(4,1)} %bitcast.180), calls=%async_computation.9 | async-start | bytes 8388608
  1022.5 26.3 %slice-start.1 = ((s8[12582912]{0:T(1024)(128)(4,1)}), s8[4194304]{0:T(1024)(128)(4,1)S(1)}, s32[]{:S(2)}) async-start(s8[12582912]{0:T(1024)(128)(4,1)} %bitcast.180), calls=%async_computation.10 | async-start | bytes 8388608
  1035.4 13.4 %slice-start.2 = ((s8[12582912]{0:T(1024)(128)(4,1)}), s8[4194304]{0:T(1024)(128)(4,1)S(1)}, s32[]{:S(2)}) async-start(s8[12582912]{0:T(1024)(128)(4,1)} %bitcast.180), calls=%async_computation.11 | async-start | bytes 8388608
  1048.8 13.3 %copy-start.9 = (s32[8,64]{1,0:T(8,128)S(1)}, s32[8,64]{1,0:T(8,128)}, u32[]{:S(2)}) copy-start(s32[8,64]{1,0:T(8,128)} %copy-done.8) | copy-start | bytes 6148
  1048.8 13.3 %copy-start.14 = (f32[8,64]{1,0:T(8,128)S(1)}, f32[8,64]{1,0:T(8,128)}, u32[]{:S(2)}) copy-start(f32[8,64]{1,0:T(8,128)} %broadcast_divide_fusion.1) | copy-start | bytes 6148
  1048.8 13.3 %copy-start.17 = (pred[8,64]{1,0:T(8,128)(4,1)S(1)}, pred[8,64]{1,0:T(8,128)(4,1)}, u32[]{:S(2)}) copy-start(pred[8,64]{1,0:T(8,128)(4,1)} %copy-done.16) | copy-start | bytes 1540
  1048.8 23.0 %copy-start.11 = (s32[64,8]{0,1:T(8,128)S(1)}, s32[64,8]{0,1:T(8,128)}, u32[]{:S(2)}) copy-start(s32[64,8]{0,1:T(8,128)} %copy-done.10) | copy-start | bytes 6148
  1062.1 20.1 %copy-start.7 = (bf16[64,512]{1,0:T(8,128)(2,1)S(1)}, bf16[64,512]{1,0:T(8,128)(2,1)}, u32[]{:S(2)}) copy-start(bf16[64,512]{1,0:T(8,128)(2,1)} %copy-done.6) | copy-start | bytes 196612
  1062.2 41.4 %copy-start.13 = (f32[512]{0:T(512)S(1)}, f32[512]{0:T(512)}, u32[]{:S(2)}) copy-start(f32[512]{0:T(512)} %copy-done.12) | copy-start | bytes 6148
  1062.2 45.8 %copy-start.15 = (f32[8,64]{1,0:T(8,128)S(1)}, f32[8,64]{1,0:T(8,128)}, u32[]{:S(2)}) copy-start(f32[8,64]{1,0:T(8,128)} %get-tuple-element.34) | copy-start | bytes 6148
  1062.2 45.8 %copy-start.22 = (f32[64]{0:T(128)S(1)}, f32[64]{0:T(128)}, u32[]{:S(2)}) copy-start(f32[64]{0:T(128)} %get-tuple-element.10) | copy-start | bytes 772
  1064.6 17.5 %all-to-all-start.4 = ((bf16[8,64,512]{2,1,0:T(8,128)(2,1)}), bf16[8,64,512]{2,1,0:T(8,128)(2,1)S(1)}, u32[]{:S(2)}, u32[]{:S(2)}) async-start(bf16[8,64,512]{2,1,0:T(8,128)(2,1)} %bitcast.177), calls=%async_computation.4 | async-start | bytes 1048576 | tf_op jit(solution)/shard_map/all_to_all | solution.py:28
  1104.5 13.1 %all-to-all-start.7 = ((bf16[8,64,512]{2,1,0:T(8,128)(2,1)}), bf16[8,64,512]{2,1,0:T(8,128)(2,1)S(1)}, u32[]{:S(2)}, u32[]{:S(2)}) async-start(bf16[8,64,512]{2,1,0:T(8,128)(2,1)} %broadcast_in_dim.130), calls=%async_computation.7 | async-start | bytes 1048576 | tf_op jit(solution)/shard_map/all_to_all | solution.py:34
  1118.4 26.1 %slice-start.3 = ((s8[12582912]{0:T(1024)(128)(4,1)}), s8[4194304]{0:T(1024)(128)(4,1)S(1)}, s32[]{:S(2)}) async-start(s8[12582912]{0:T(1024)(128)(4,1)} %bitcast.182), calls=%async_computation.12 | async-start | bytes 8388608
  1118.4 26.1 %slice-start.4 = ((s8[12582912]{0:T(1024)(128)(4,1)}), s8[4194304]{0:T(1024)(128)(4,1)S(1)}, s32[]{:S(2)}) async-start(s8[12582912]{0:T(1024)(128)(4,1)} %bitcast.182), calls=%async_computation.13 | async-start | bytes 8388608
  1131.3 13.2 %slice-start.5 = ((s8[12582912]{0:T(1024)(128)(4,1)}), s8[4194304]{0:T(1024)(128)(4,1)S(1)}, s32[]{:S(2)}) async-start(s8[12582912]{0:T(1024)(128)(4,1)} %bitcast.182), calls=%async_computation.14 | async-start | bytes 8388608
  1144.5 19.3 %copy-start.5 = (f32[3,8,12,32]{3,2,1,0:T(8,128)S(1)}, f32[3,8,12,32]{3,2,1,0:T(8,128)}, u32[]{:S(2)}) copy-start(f32[3,8,12,32]{3,2,1,0:T(8,128)} %copy-done.4) | copy-start | bytes 110596
  1144.5 29.6 %copy-start.1 = (bf16[8,256,512]{2,1,0:T(8,128)(2,1)S(1)}, bf16[8,256,512]{2,1,0:T(8,128)(2,1)}, u32[]{:S(2)}) copy-start(bf16[8,256,512]{2,1,0:T(8,128)(2,1)} %param.16) | copy-start | bytes 6291460
  1160.3 13.1 %all-to-all-start.8 = ((bf16[8,64,512]{2,1,0:T(8,128)(2,1)}), bf16[8,64,512]{2,1,0:T(8,128)(2,1)S(1)}, u32[]{:S(2)}, u32[]{:S(2)}) async-start(bf16[8,64,512]{2,1,0:T(8,128)(2,1)} %bitcast.173), calls=%async_computation.8 | async-start | bytes 1048576 | tf_op jit(solution)/shard_map/all_to_all | solution.py:28
